TPU v7x, 32 devices: a whole 2x2x4 slice. The times are simulated.
32 devices in a mesh: dp: 16 (over z, y, x), tensor: 2 (over core).
Axes of the slice: x: 2, y: 2, z: 4, core: 2. Of those that a mesh axis runs over, the one named last changes fastest.
Arguments:
- tokens: float32 [16384, 768], P(('dp', 'tensor')), may hold values from -6 to 6
- offsets: int32 [16, 16], P('dp'), may hold values from 0 to 1024, as said below
- w_qkv: bfloat16 [768, 3, 768], P('dp', None, 'tensor'), may hold values from -0.21875 to 0.21875
- w_attn_out: bfloat16 [768, 768], P('tensor', 'dp'), may hold values from -1.75 to 1.75
- w_in: bfloat16 [768, 2, 1152], P('dp', None, 'tensor'), may hold values from -0.21875 to 0.21875
- w_mlp_out: bfloat16 [1152, 768], P('tensor', 'dp'), may hold values from -0.1875 to 0.1875
- gain_attn: bfloat16 [768], P('dp'), may hold values from 0.099609375 to 1.8984375
- gain_mlp: bfloat16 [768], P('dp'), may hold values from 0.099609375 to 1.8984375
- cotangent: float32 [16384, 768], P(('dp', 'tensor')), may hold values from -6 to 6
Outputs:
- outputs: float32 [16384, 768], P(('dp', 'tensor'))
- grad_tokens: float32 [16384, 768], P(('dp', 'tensor'))
- grad_w_qkv: float32 [768, 3, 768], P('dp', None, 'tensor')
- grad_w_attn_out: float32 [768, 768], P('tensor', 'dp')
- grad_w_in: float32 [768, 2, 1152], P('dp', None, 'tensor')
- grad_w_mlp_out: float32 [1152, 768], P('tensor', 'dp')
- grad_gain_attn: float32 [768], P('dp')
- grad_gain_mlp: float32 [768], P('dp')
Inputs may be any that keep to these rules, and one draw needn't show every extreme that they name: `offsets`: each row holds the first tokens of 16 sequences of one group of 1024 tokens, rising from 0 and never falling (equal entries are empty sequences); a sequence ends where the next begins, the last at 1024. No sequence has more than 512 tokens; in every row one has exactly 512 and holds the group's tokens 512 - 1 and 512.
All inputs are finite; a program needn't handle non-finite values.
Results may differ from a plain program's by a relative error of at most 0.018.
Values may be sent and summed in bfloat16 or wider, within the bound.
A program may use at most 128 MiB of HBM per device.

v0:
```python
import math
import jax
import jax.numpy as jnp
from jax import lax
from jax.sharding import PartitionSpec as P

HEAD_DIM = 64
EPSILON = 1e-05
ROPE_BASE = 160000.0
NEGATIVE = -1e30


def seq_starts(offset_row, count_rows):
    position = jnp.arange(count_rows, dtype=jnp.int32)
    before = offset_row[None, :] <= position[:, None]
    return jnp.max(jnp.where(before, offset_row[None, :], 0), axis=1)


def rope_tables(starts):
    count_rows = starts.shape[0]
    position = jnp.arange(count_rows, dtype=jnp.int32) - starts
    half_dim = HEAD_DIM // 2
    inverse = jnp.power(
        jnp.float32(ROPE_BASE), -2.0 * jnp.arange(half_dim, dtype=jnp.float32) / HEAD_DIM
    )
    angles = position.astype(jnp.float32)[:, None] * inverse[None, :]
    return (jnp.cos(angles), jnp.sin(angles))


def rotate(head_rows, cosine_tab, sine_tab):
    half_dim = HEAD_DIM // 2
    first_half = head_rows[..., :half_dim]
    second = head_rows[..., half_dim:]
    cosine_b = cosine_tab[:, None, :]
    sine_b = sine_tab[:, None, :]
    return jnp.concatenate(
        [first_half * cosine_b - second * sine_b, second * cosine_b + first_half * sine_b], axis=-1
    )


def rotate_back(head_grads, cosine_tab, sine_tab):
    half_dim = HEAD_DIM // 2
    first_half = head_grads[..., :half_dim]
    second = head_grads[..., half_dim:]
    cosine_b = cosine_tab[:, None, :]
    sine_b = sine_tab[:, None, :]
    return jnp.concatenate(
        [first_half * cosine_b + second * sine_b, second * cosine_b - first_half * sine_b], axis=-1
    )


def layer_norm(inputs_v, gain_v):
    centre = inputs_v - jnp.mean(inputs_v, axis=-1, keepdims=True)
    spread = jnp.mean(centre * centre, axis=-1, keepdims=True)
    return centre * lax.rsqrt(spread + EPSILON) * gain_v


def exact_gelu(gate_in):
    return jax.nn.gelu(gate_in, approximate=False)


def fetch_attention(w_qkv, w_attn_out, gain_attn):
    return (
        lax.all_gather(w_qkv, "dp", axis=0, tiled=True),
        lax.all_gather(w_attn_out, "dp", axis=1, tiled=True),
        lax.all_gather(gain_attn, "dp", axis=0, tiled=True),
    )


def fetch_attention_again(w_qkv, w_attn_out, gain_attn):
    return (
        lax.all_gather(w_qkv, "dp", axis=0, tiled=True),
        lax.all_gather(w_attn_out, "dp", axis=1, tiled=True),
        lax.all_gather(gain_attn, "dp", axis=0, tiled=True),
    )


def fetch_mlp(w_in, w_mlp_out, gain_mlp):
    return (
        lax.all_gather(w_in, "dp", axis=0, tiled=True),
        lax.all_gather(w_mlp_out, "dp", axis=1, tiled=True),
        lax.all_gather(gain_mlp, "dp", axis=0, tiled=True),
    )


def fetch_mlp_again(w_in, w_mlp_out, gain_mlp):
    return (
        lax.all_gather(w_in, "dp", axis=0, tiled=True),
        lax.all_gather(w_mlp_out, "dp", axis=1, tiled=True),
        lax.all_gather(gain_mlp, "dp", axis=0, tiled=True),
    )


def spread_rows(local_rows):
    return lax.all_gather(local_rows, "tensor", axis=0, tiled=True)


def spread_grads(local_rows):
    return lax.all_gather(local_rows, "tensor", axis=0, tiled=True)


def collect_rows(inputs_all, weight_full, rows_here):

    def term_of(row_start, row_count):
        return jnp.dot(inputs_all, weight_full, preferred_element_type=jnp.float32)

    return lax.psum_scatter(
        term_of(jnp.int32(0), rows_here * lax.axis_size("tensor")).astype(jnp.bfloat16),
        "tensor",
        scatter_dimension=0,
        tiled=True,
    ).astype(jnp.float32)


def collect_grads(grads_all, weight_full, rows_here):

    def term_of(row_start, row_count):
        return jnp.einsum("tsk,dsk->td", grads_all, weight_full, preferred_element_type=jnp.float32)

    return lax.psum_scatter(
        term_of(jnp.int32(0), rows_here * lax.axis_size("tensor")).astype(jnp.bfloat16),
        "tensor",
        scatter_dimension=0,
        tiled=True,
    ).astype(jnp.float32)


def block_scores(query_block, start_block, key_rows, starts, scale_factor):
    raw_scores = (
        jnp.einsum("qhe,khe->hqk", query_block, key_rows, preferred_element_type=jnp.float32)
        * scale_factor
    )
    same_seq = start_block[:, None] == starts[None, :]
    return jnp.where(same_seq[None], raw_scores, NEGATIVE)


def attention_forward(queries, key_rows, values, starts, scale_factor):
    group_rows, heads_here, head_dim = queries.shape
    block_rows = min(512, group_rows)
    block_count = group_rows // block_rows

    def one_block(block_in):
        query_block, start_block = block_in
        masked = block_scores(query_block, start_block, key_rows, starts, scale_factor)
        row_max = jnp.max(masked, axis=-1, keepdims=True)
        exp_terms = jnp.exp(masked - row_max)
        row_total = jnp.sum(exp_terms, axis=-1, keepdims=True)
        softmax_w = exp_terms / row_total
        mixed_out = jnp.einsum(
            "hqk,khe->qhe",
            softmax_w.astype(jnp.bfloat16),
            values,
            preferred_element_type=jnp.float32,
        )
        return (mixed_out, (row_max + jnp.log(row_total))[..., 0])

    mixed_all, lse_stack = lax.map(
        one_block,
        (
            queries.reshape(block_count, block_rows, heads_here, head_dim),
            starts.reshape(block_count, block_rows),
        ),
    )
    return (mixed_all.reshape(group_rows, heads_here, head_dim), lse_stack)


def attention_backward(queries, key_rows, values, starts, lse_stack, grad_out, scale_factor):
    group_rows, heads_here, head_dim = queries.shape
    block_rows = min(512, group_rows)
    block_count = group_rows // block_rows

    def one_block(carry_in, block_in):
        grad_keys, grad_values = carry_in
        query_block, start_block, lse_block, grad_block = block_in
        masked = block_scores(query_block, start_block, key_rows, starts, scale_factor)
        softmax_w = jnp.exp(masked - lse_block[..., None])
        grad_values = grad_values + jnp.einsum(
            "hqk,qhe->khe",
            softmax_w.astype(jnp.bfloat16),
            grad_block,
            preferred_element_type=jnp.float32,
        )
        grad_probs = jnp.einsum(
            "qhe,khe->hqk", grad_block, values, preferred_element_type=jnp.float32
        )
        grad_scores = softmax_w * (
            grad_probs - jnp.sum(softmax_w * grad_probs, axis=-1, keepdims=True)
        )
        rounded = grad_scores.astype(jnp.bfloat16)
        grad_query = (
            jnp.einsum("hqk,khe->qhe", rounded, key_rows, preferred_element_type=jnp.float32)
            * scale_factor
        )
        grad_keys = (
            grad_keys
            + jnp.einsum("hqk,qhe->khe", rounded, query_block, preferred_element_type=jnp.float32)
            * scale_factor
        )
        return ((grad_keys, grad_values), grad_query)

    zero_grads = jnp.zeros((group_rows, heads_here, head_dim), jnp.float32)
    block_inputs = (
        queries.reshape(block_count, block_rows, heads_here, head_dim),
        starts.reshape(block_count, block_rows),
        lse_stack,
        grad_out.reshape(block_count, block_rows, heads_here, head_dim),
    )
    (grad_keys, grad_values), grad_queries = lax.scan(
        one_block, (zero_grads, zero_grads), block_inputs
    )
    return (grad_queries.reshape(group_rows, heads_here, head_dim), grad_keys, grad_values)


def shards(tokens, offsets, w_qkv, w_attn_out, w_in, w_mlp_out, gain_attn, gain_mlp, cotangent):
    rows_here = tokens.shape[0]
    group_rows = rows_here * lax.axis_size("tensor")
    scale_factor = 1.0 / math.sqrt(HEAD_DIM)
    starts = seq_starts(offsets[0], group_rows)
    cosine_tab, sine_tab = rope_tables(starts)
    qkv_full, attn_out_full, gain_one_low = fetch_attention(w_qkv, w_attn_out, gain_attn)
    gain_one = gain_one_low.astype(jnp.float32)
    normed_all = spread_rows(layer_norm(tokens, gain_one).astype(jnp.bfloat16))
    projected = jnp.einsum("td,dsk->tsk", normed_all, qkv_full, preferred_element_type=jnp.float32)
    width_here = projected.shape[2]
    heads_here = width_here // HEAD_DIM
    split_heads = projected.reshape(group_rows, 3, heads_here, HEAD_DIM)
    queries = rotate(split_heads[:, 0], cosine_tab, sine_tab).astype(jnp.bfloat16)
    key_rows = rotate(split_heads[:, 1], cosine_tab, sine_tab).astype(jnp.bfloat16)
    values = split_heads[:, 2].astype(jnp.bfloat16)
    mixed_all, lse_stack = attention_forward(queries, key_rows, values, starts, scale_factor)
    context = mixed_all.reshape(group_rows, width_here).astype(jnp.bfloat16)
    attended = collect_rows(context, attn_out_full, rows_here)
    hidden = tokens + attended
    mlp_in_full, mlp_out_full, gain_two_low = fetch_mlp(w_in, w_mlp_out, gain_mlp)
    gain_two = gain_two_low.astype(jnp.float32)
    mlp_normed = layer_norm(hidden, gain_two).astype(jnp.bfloat16)
    mlp_in_use, mlp_out_use = (mlp_in_full, mlp_out_full)
    mlp_rows = spread_rows(mlp_normed)
    gate_up = jnp.einsum("td,dsf->tsf", mlp_rows, mlp_in_use, preferred_element_type=jnp.float32)
    gate_part = gate_up[:, 0]
    up_part = gate_up[:, 1]
    activated = exact_gelu(gate_part)
    product_rows = (activated * up_part).astype(jnp.bfloat16)
    branch = collect_rows(product_rows, mlp_out_use, rows_here)
    outputs = hidden + branch
    mlp_in_back, mlp_out_back, gain_two_again = fetch_mlp_again(w_in, w_mlp_out, gain_mlp)
    gain_two_back = gain_two_again.astype(jnp.float32)
    grad_rows = spread_grads(cotangent.astype(jnp.bfloat16))
    grad_mlp_out = jnp.einsum(
        "tf,td->fd", product_rows, grad_rows, preferred_element_type=jnp.float32
    )
    grad_product = jnp.einsum(
        "td,fd->tf", grad_rows, mlp_out_back, preferred_element_type=jnp.float32
    )
    unused_out, gelu_pull = jax.vjp(exact_gelu, gate_part)
    grad_gate = gelu_pull(grad_product * up_part)[0]
    grad_up = grad_product * activated
    grad_gate_up = jnp.stack([grad_gate, grad_up], axis=1).astype(jnp.bfloat16)
    grad_mlp_in = jnp.einsum(
        "td,tsf->dsf", mlp_rows, grad_gate_up, preferred_element_type=jnp.float32
    )
    grad_normed_two = collect_grads(grad_gate_up, mlp_in_back, rows_here)
    unused_two, norm_pull_two = jax.vjp(layer_norm, hidden, gain_two_back)
    grad_hidden_norm, grad_gain_two = norm_pull_two(grad_normed_two)
    grad_hidden = cotangent + grad_hidden_norm
    mlp_sums = (
        lax.psum_scatter(grad_mlp_in, "dp", scatter_dimension=0, tiled=True),
        lax.psum_scatter(grad_mlp_out, "dp", scatter_dimension=1, tiled=True),
        lax.psum_scatter(grad_gain_two, "dp", scatter_dimension=0, tiled=True),
    )
    qkv_back, attn_out_back, gain_one_again = fetch_attention_again(w_qkv, w_attn_out, gain_attn)
    gain_one_back = gain_one_again.astype(jnp.float32)
    grad_hidden_rows = spread_grads(grad_hidden.astype(jnp.bfloat16))
    grad_attn_out = jnp.einsum(
        "te,td->ed", context, grad_hidden_rows, preferred_element_type=jnp.float32
    )
    grad_context = jnp.einsum(
        "td,ed->te", grad_hidden_rows, attn_out_back, preferred_element_type=jnp.float32
    ).astype(jnp.bfloat16)
    grad_queries, grad_keys, grad_values = attention_backward(
        queries,
        key_rows,
        values,
        starts,
        lse_stack,
        grad_context.reshape(group_rows, heads_here, HEAD_DIM),
        scale_factor,
    )
    grad_projected = jnp.stack(
        [
            rotate_back(grad_queries, cosine_tab, sine_tab),
            rotate_back(grad_keys, cosine_tab, sine_tab),
            grad_values,
        ],
        axis=1,
    )
    grad_projected = grad_projected.reshape(group_rows, 3, width_here).astype(jnp.bfloat16)
    grad_qkv = jnp.einsum(
        "td,tsk->dsk", normed_all, grad_projected, preferred_element_type=jnp.float32
    )
    grad_normed_one = collect_grads(grad_projected, qkv_back, rows_here)
    unused_one, norm_pull_one = jax.vjp(layer_norm, tokens, gain_one_back)
    grad_tokens_norm, grad_gain_one = norm_pull_one(grad_normed_one)
    grad_tokens = grad_hidden + grad_tokens_norm
    attn_sums = (
        lax.psum_scatter(grad_qkv, "dp", scatter_dimension=0, tiled=True),
        lax.psum_scatter(grad_attn_out, "dp", scatter_dimension=1, tiled=True),
        lax.psum_scatter(grad_gain_one, "dp", scatter_dimension=0, tiled=True),
    )
    shard_mlp_in, shard_mlp_out, shard_gain_two = mlp_sums
    shard_qkv, shard_attn_out, shard_gain_one = attn_sums
    gain_one_total, gain_two_total = lax.psum((shard_gain_one, shard_gain_two), "tensor")
    return (
        outputs,
        grad_tokens,
        shard_qkv,
        shard_attn_out,
        shard_mlp_in,
        shard_mlp_out,
        gain_one_total,
        gain_two_total,
    )


def solution(mesh):
    in_specs = (
        P(("dp", "tensor"), None),
        P("dp", None),
        P("dp", None, "tensor"),
        P("tensor", "dp"),
        P("dp", None, "tensor"),
        P("tensor", "dp"),
        P("dp"),
        P("dp"),
        P(("dp", "tensor"), None),
    )
    out_specs = (
        P(("dp", "tensor"), None),
        P(("dp", "tensor"), None),
        P("dp", None, "tensor"),
        P("tensor", "dp"),
        P("dp", None, "tensor"),
        P("tensor", "dp"),
        P("dp"),
        P("dp"),
    )
    return jax.shard_map(shards, mesh=mesh, in_specs=in_specs, out_specs=out_specs, check_vma=False)
```

profile of v0, /device:TPU:0, one launch (start us, length us, event | category | flops | bytes accessed | tf_op | source)
XLA Modules:
  0.0 875.3 jit_solution(12923273058877242758)
XLA Ops:
  11.2 43.5 %all-reduce.6 = (bf16[768]{0:T(1024)(128)(2,1)S(1)}, bf16[768]{0:T(1024)(128)(2,1)S(1)}) all-reduce(bf16[768]{0:T(1024)(128)(2,1)S(1)} %dynamic-update-slice, bf16[768]{0:T(1024)(128)(2,1)S(1)} %dynamic-update-slice.1), channel_id=1, replica_groups=mesh['dp'=16,'tensor'=2] {'dp'}, use_global_device_ids=true, to_apply=%add | all-reduce | flops 1536 | bytes 6144
  57.4 41.6 %all_gather.39 = bf16[384,768]{0,1:T(8,128)(2,1)} all-gather(bf16[384,48]{0,1:T(8,128)(2,1)S(1)} %copy-done.31), channel_id=1, replica_groups=mesh['dp'=16,'tensor'=2] {'dp'}, dimensions={1}, use_global_device_ids=true | all-gather | bytes 626688 | tf_op jit(solution)/shard_map/all_gather | solution.py:65
  99.1 25.5 %all-gather.9.cloned.1.call-done = bf16[768,3,384]{2,0,1:T(8,128)(2,1)} async-done(((bf16[48,3,384]{2,0,1:T(8,128)(2,1)}), bf16[768,3,384]{2,0,1:T(8,128)(2,1)}) %all-gather.9.cloned.1.call-update) | async-done | bytes 1769488 | tf_op jit(solution)/shard_map/all_gather | solution.py:64
  132.2 25.0 %while.27 = (s32[]{:T(128)}, bf16[2,512,6,64]{1,3,2,0:T(8,128)(2,1)S(1)}, f32[2,6,512]{2,1,0:T(8,128)S(1)}, s32[2,512]{1,0:T(2,128)S(1)}, s32[1024]{0:T(1024)S(1...) while((s32[]{:T(128)}, ...), condition=%wide.region_6.7_spmd, body=%wide.region_3.6_spmd.sunk | while | flops 843576320 | bytes 42727540 | solution.py:157
  139.6 5.1 fusion.131
  152.2 5.1 fusion.131
  164.6 4.7 reduce-scatter.9.cloned.1.call-done
  173.0 51.0 %all_gather.43 = bf16[576,768]{0,1:T(8,128)(2,1)} all-gather(bf16[576,48]{0,1:T(8,128)(2,1)S(1)} %copy-done.30), channel_id=1, replica_groups=mesh['dp'=16,'tensor'=2] {'dp'}, dimensions={1}, use_global_device_ids=true | all-gather | bytes 940032 | tf_op jit(solution)/shard_map/all_gather | solution.py:81
  226.9 20.7 %all-gather.13.cloned.1.call-done = bf16[768,2,576]{2,0,1:T(8,128)(2,1)} async-done(((bf16[48,2,576]{2,0,1:T(8,128)(2,1)}), bf16[768,2,576]{2,0,1:T(8,128)(2,1)}) %all-gather.13.cloned.1.call-update) | async-done | bytes 1769488 | tf_op jit(solution)/shard_map/all_gather | solution.py:80
  247.6 10.5 %all-gather.11.cloned.1.call-done = bf16[1024,768]{1,0:T(8,128)(2,1)} async-done(((bf16[512,768]{1,0:T(8,128)(2,1)}), bf16[1024,768]{1,0:T(8,128)(2,1)}) %all-gather.11.cloned.1.call-update) | async-done | bytes 1572880 | tf_op jit(solution)/shard_map/all_gather | solution.py:95
  262.3 5.6 fusion.71
  277.6 7.6 reduce-scatter.13.cloned.1.call-done
  287.7 10.0 %reduce-scatter.11.cloned.1.call-done = bf16[512,768]{1,0:T(8,128)(2,1)} async-done(((bf16[1024,768]{1,0:T(8,128)(2,1)}), bf16[512,768]{1,0:T(8,128)(2,1)}) %reduce-scatter.11.cloned.1.call-update) | async-done | bytes 786448 | tf_op jit(solution)/shard_map/reduce_scatter | solution.py:107
  303.6 5.8 fusion.62
  309.5 4.8 all-gather.17.cloned.1.call-done
  322.7 89.6 %while.28 = (s32[]{:T(128)}, f32[1024,6,64]{0,2,1:T(8,128)S(1)}, f32[1024,6,64]{0,2,1:T(8,128)}, f32[2,512,6,64]{1,0,3,2:T(2,128)}, bf16[2,512,6,64]{1,3,2,0:T(8...) while((s32[]{:T(128)}, f32[1024,6,64]{0,2,1:T(8,128)S(1)}, ...), condition=%wide.region_16.17_spmd.clone, body=%wide.region_14.16_spmd.clone.sunk | while | flops 2063135744 | bytes 110721200 | solution.py:208
  326.1 5.5 bitcast_add_fusion.5
  331.6 8.4 multiply_reduce_fusion.4
  340.0 7.0 multiply_convert_fusion.6
  352.2 15.0 %dynamic_update_slice.19 = f32[2,512,6,64]{1,0,3,2:T(2,128)} dynamic-update-slice(f32[2,512,6,64]{1,0,3,2:T(2,128)} %get-tuple-element.475, f32[1,512,6,64]{1,0,3,2:T(1,128)S(1)} %copy.88, s32[]{:T(128)S(6)} %copy.108, s32[]{:T(128)} %constant.64.clone.1..sunk, s32[]{:T(128)} %constant.64.clone.1..sunk, s32[]{:T(128)} %constant.64.clone.1..sunk) | dynamic-update-slice | bytes 1572868 | tf_op jit(solution)/shard_map/while/body/jit(dynamic_update_index_in_dim)/dynamic_update_slice | solution.py:157
  370.5 6.1 bitcast_add_fusion.5
  376.5 8.5 multiply_reduce_fusion.4
  385.0 6.9 multiply_convert_fusion.6
  397.1 15.0 %dynamic_update_slice.19 = f32[2,512,6,64]{1,0,3,2:T(2,128)} dynamic-update-slice(f32[2,512,6,64]{1,0,3,2:T(2,128)} %get-tuple-element.475, f32[1,512,6,64]{1,0,3,2:T(1,128)S(1)} %copy.88, s32[]{:T(128)S(6)} %copy.108, s32[]{:T(128)} %constant.64.clone.1..sunk, s32[]{:T(128)} %constant.64.clone.1..sunk, s32[]{:T(128)} %constant.64.clone.1..sunk) | dynamic-update-slice | bytes 1572868 | tf_op jit(solution)/shard_map/while/body/jit(dynamic_update_index_in_dim)/dynamic_update_slice | solution.py:157
  421.3 5.2 bitcast_convert_fusion
  434.6 5.4 fusion.66
  440.8 16.0 %reduce-scatter.21.cloned.1.call-done = f32[48,2,576]{2,0,1:T(8,128)} async-done(((f32[768,2,576]{2,0,1:T(8,128)}), f32[48,2,576]{2,0,1:T(8,128)}) %reduce-scatter.21.cloned.1.call-update) | async-done | bytes 221200 | tf_op jit(solution)/shard_map/reduce_scatter | solution.py:267
  458.6 9.5 %reduce-scatter.15.cloned.1.call-done = bf16[512,768]{1,0:T(8,128)(2,1)} async-done(((bf16[1024,768]{1,0:T(8,128)(2,1)}), bf16[512,768]{1,0:T(8,128)(2,1)}) %reduce-scatter.15.cloned.1.call-update) | async-done | bytes 786448 | tf_op jit(solution)/shard_map/reduce_scatter | solution.py:120
  470.6 42.8 %all-reduce.4 = (f32[768]{0:T(1024)S(1)}, f32[768]{0:T(1024)S(1)}) all-reduce(f32[768]{0:T(1024)S(1)} %get-tuple-element.227, f32[768]{0:T(1024)S(1)} %copy-done.38), channel_id=10, replica_groups=mesh['dp'=16,'tensor'=2] {'dp'}, use_global_device_ids=true, to_apply=%region_25.26.clone | all-reduce | flops 1536 | bytes 12288
  520.2 80.6 %reduce-scatter.23.cloned.1.call-done = f32[576,48]{0,1:T(8,128)} async-done(((f32[576,768]{0,1:T(8,128)}), f32[576,48]{0,1:T(8,128)}) %reduce-scatter.23.cloned.1.call-update) | async-done | bytes 110608 | tf_op jit(solution)/shard_map/reduce_scatter | solution.py:268
  600.8 128.6 %reduce-scatter.19.cloned.1.call-done = f32[384,48]{0,1:T(8,128)} async-done(((f32[384,768]{0,1:T(8,128)}), f32[384,48]{0,1:T(8,128)}) %reduce-scatter.19.cloned.1.call-update) | async-done | bytes 73744 | tf_op jit(solution)/shard_map/reduce_scatter | solution.py:307
  729.4 138.9 %reduce-scatter.17.cloned.1.call-done = f32[48,3,384]{2,0,1:T(8,128)} async-done(((f32[768,3,384]{2,0,1:T(8,128)}), f32[48,3,384]{2,0,1:T(8,128)}) %reduce-scatter.17.cloned.1.call-update) | async-done | bytes 221200 | tf_op jit(solution)/shard_map/reduce_scatter | solution.py:306
  (213 shorter events, 117.4 us)
Async XLA Ops:
  7.2 91.8 %all-gather.7.cloned.1.call-start = ((), (), s32[]{:S(2)}) async-start(), calls=%async_computation.8 | async-start | bytes 2359296 | tf_op jit(solution)/shard_map/all_gather | solution.py:95
  9.1 46.8 %copy-start.28 = (f32[512]{0:T(512)}, f32[512]{0:T(512)S(1)}, u32[]{:S(2)}) copy-start(f32[512]{0:T(512)S(1)} %broadcast_multiply_fusion.1) | copy-start | bytes 6148
  9.1 47.6 %copy-start.40 = (s32[1,16]{1,0:T(1,128)S(1)}, s32[1,16]{1,0:T(1,128)}, u32[]{:S(2)}) copy-start(s32[1,16]{1,0:T(1,128)} %param.14) | copy-start | bytes 196
  9.1 48.3 %copy-start.31 = (bf16[384,48]{0,1:T(8,128)(2,1)S(1)}, bf16[384,48]{0,1:T(8,128)(2,1)}, u32[]{:S(2)}) copy-start(bf16[384,48]{0,1:T(8,128)(2,1)} %param.16) | copy-start | bytes 110596
  9.4 45.3 %copy-start.36 = (f32[512]{0:T(512)}, f32[512]{0:T(512)S(1)}, u32[]{:S(2)}) copy-start(f32[512]{0:T(512)S(1)} %multiply_reduce_fusion.2) | copy-start | bytes 6148
  9.4 47.4 %copy-start.32 = (f32[512]{0:T(512)}, f32[512]{0:T(512)S(1)}, u32[]{:S(2)}) copy-start(f32[512]{0:T(512)S(1)} %fusion.74) | copy-start | bytes 6148
  55.9 68.7 %all-gather.9.cloned.1.call-start = ((), (), s32[]{:S(2)}) async-start(), calls=%async_computation.9 | async-start | bytes 1880064 | tf_op jit(solution)/shard_map/all_gather | solution.py:64
  56.6 112.7 %reduce-scatter.9.cloned.1.call-start = ((), (), s32[]{:S(2)}) async-start(), calls=%async_computation.10 | async-start | bytes 2359296 | tf_op jit(solution)/shard_map/reduce_scatter | solution.py:107
  57.4 72.6 %copy-start.12 = (f32[1024,32]{0,1:T(8,128)}, f32[1024,32]{0,1:T(8,128)S(1)}, u32[]{:S(2)}) copy-start(f32[1024,32]{0,1:T(8,128)S(1)} %get-tuple-element.302) | copy-start | bytes 393220
  57.4 72.6 %copy-start.14 = (f32[1024,32]{0,1:T(8,128)}, f32[1024,32]{0,1:T(8,128)S(1)}, u32[]{:S(2)}) copy-start(f32[1024,32]{0,1:T(8,128)S(1)} %get-tuple-element.303) | copy-start | bytes 393220
  161.3 62.8 %all-gather.15.cloned.1.call-start = ((), (), s32[]{:S(2)}) async-start(), calls=%async_computation.14 | async-start | bytes 2359296 | tf_op jit(solution)/shard_map/all_gather | solution.py:99
  163.8 83.8 %all-gather.13.cloned.1.call-start = ((), (), s32[]{:S(2)}) async-start(), calls=%async_computation.12 | async-start | bytes 2088960 | tf_op jit(solution)/shard_map/all_gather | solution.py:80
  164.5 93.6 %all-gather.11.cloned.1.call-start = ((), (), s32[]{:S(2)}) async-start(), calls=%async_computation.11 | async-start | bytes 2359296 | tf_op jit(solution)/shard_map/all_gather | solution.py:95
  173.0 112.2 %reduce-scatter.13.cloned.1.call-start = ((), (), s32[]{:S(2)}) async-start(), calls=%async_computation.15 | async-start | bytes 2359296 | tf_op jit(solution)/shard_map/reduce_scatter | solution.py:120
  274.8 22.9 %reduce-scatter.11.cloned.1.call-start = ((), (), s32[]{:S(2)}) async-start(), calls=%async_computation.13 | async-start | bytes 2359296 | tf_op jit(solution)/shard_map/reduce_scatter | solution.py:107
  277.5 7.7 copy-start.3
  277.6 36.7 %all-gather.17.cloned.1.call-start = ((), (), s32[]{:S(2)}) async-start(), calls=%async_computation.16 | async-start | bytes 2359296 | tf_op jit(solution)/shard_map/all_gather | solution.py:99
  285.2 12.5 %copy-start.7 = (bf16[512,768]{1,0:T(8,128)(2,1)S(1)}, bf16[512,768]{1,0:T(8,128)(2,1)}, u32[]{:S(2)}) copy-start(bf16[512,768]{1,0:T(8,128)(2,1)} %reduce-scatter.13.cloned.1.call-done) | copy-start | bytes 2359300
  303.1 153.7 %reduce-scatter.21.cloned.1.call-start = ((), (), s32[]{:S(2)}) async-start(), calls=%async_computation.20 | async-start | bytes 4177920 | tf_op jit(solution)/shard_map/reduce_scatter | solution.py:267
  309.4 158.6 %reduce-scatter.15.cloned.1.call-start = ((), (), s32[]{:S(2)}) async-start(), calls=%async_computation.17 | async-start | bytes 2359296 | tf_op jit(solution)/shard_map/reduce_scatter | solution.py:120
  317.6 5.1 copy-start.24
  421.3 5.3 copy-start.9
  426.6 174.3 %reduce-scatter.23.cloned.1.call-start = ((), (), s32[]{:S(2)}) async-start(), calls=%async_computation.21 | async-start | bytes 2088960 | tf_op jit(solution)/shard_map/reduce_scatter | solution.py:268
  430.9 298.5 %reduce-scatter.19.cloned.1.call-start = ((), (), s32[]{:S(2)}) async-start(), calls=%async_computation.19 | async-start | bytes 1253376 | tf_op jit(solution)/shard_map/reduce_scatter | solution.py:307
  434.6 433.8 %reduce-scatter.17.cloned.1.call-start = ((), (), s32[]{:S(2)}) async-start(), calls=%async_computation.18 | async-start | bytes 3760128 | tf_op jit(solution)/shard_map/reduce_scatter | solution.py:306
  440.0 28.0 %copy-start.1 = (f32[512,768]{1,0:T(8,128)S(1)}, f32[512,768]{1,0:T(8,128)}, u32[]{:S(2)}) copy-start(f32[512,768]{1,0:T(8,128)} %param.13) | copy-start | bytes 4718596
  440.0 28.0 %copy-start.27 = (f32[768]{0:T(1024)S(1)}, f32[768]{0:T(1024)}, u32[]{:S(2)}) copy-start(f32[768]{0:T(1024)} %copy-done.26) | copy-start | bytes 9220
  440.0 28.0 %copy-start.29 = (f32[512]{0:T(512)S(1)}, f32[512]{0:T(512)}, u32[]{:S(2)}) copy-start(f32[512]{0:T(512)} %copy-done.28) | copy-start | bytes 6148
  440.0 29.6 %copy-start.37 = (f32[512]{0:T(512)S(1)}, f32[512]{0:T(512)}, u32[]{:S(2)}) copy-start(f32[512]{0:T(512)} %copy-done.36) | copy-start | bytes 6148
  440.1 29.6 %copy-start.33 = (f32[512]{0:T(512)S(1)}, f32[512]{0:T(512)}, u32[]{:S(2)}) copy-start(f32[512]{0:T(512)} %copy-done.32) | copy-start | bytes 6148
  458.6 12.0 %copy-start.38 = (f32[768]{0:T(1024)S(1)}, f32[768]{0:T(1024)}, u32[]{:S(2)}) copy-start(f32[768]{0:T(1024)} %get-tuple-element.229) | copy-start | bytes 9220
  458.6 57.9 %copy-start.35 = (f32[512]{0:T(512)S(1)}, f32[512]{0:T(512)}, u32[]{:S(2)}) copy-start(f32[512]{0:T(512)} %copy-done.34) | copy-start | bytes 6148
  (26 other events, 70.2 us)
Sparse Core Ops, SparseCore 0:
  56.0 5.6 all-gather.6
  64.4 60.1 all-gather.8
  161.4 7.8 reduce-scatter.8
  170.8 10.9 all-gather.14
  185.3 62.2 all-gather.12
  249.7 8.4 all-gather.10
  274.9 10.2 reduce-scatter.12
  287.4 10.2 reduce-scatter.10
  303.3 10.9 all-gather.16
  320.1 136.6 reduce-scatter.20
  459.7 8.2 reduce-scatter.14
  473.3 127.4 reduce-scatter.22
  606.9 122.5 reduce-scatter.18
  735.8 132.5 reduce-scatter.16
where the time goes:
time: 888 us; the launch traced here: 875 us
  waiting for transfers between devices  458 us (52%)
  blocking collectives  182 us (20%)
  matrix products  107 us (12%)
  other arithmetic  56.4 us (6%)
  local copies, waits for them, and re-layouts  54.4 us (6%)
  between operations  16.3 us (2%)
    reduce_scatter x1, waiting for transfers between devices, shards(): lax.psum_scatter(grad_qkv, 'dp', scatter_dimension=0, tiled=True)  139 us
    reduce_scatter x1, waiting for transfers between devices, shards(): lax.psum_scatter(grad_attn_out, 'dp', scatter_dimension=1, tiled=True)  129 us
    unnamed x2, blocking collectives  86.3 us
    reduce_scatter x1, waiting for transfers between devices, shards(): lax.psum_scatter(grad_mlp_out, 'dp', scatter_dimension=1, tiled=True)  80.6 us
    all_gather x1, blocking collectives, fetch_mlp(): lax.all_gather(w_mlp_out, 'dp', axis=1, tiled=True)  51 us
    all_gather x1, blocking collectives, fetch_attention(): lax.all_gather(w_attn_out, 'dp', axis=1, tiled=True)  41.6 us
    dynamic_update_slice x4, local copies, waits for them, and re-layouts, attention_forward(): lax.map(one_block, (queries.reshape(block_count, block_rows, heads_here,...  31.7 us
    all_gather x1, waiting for transfers between devices, fetch_attention(): lax.all_gather(w_qkv, 'dp', axis=0, tiled=True)  25.5 us
  transfers between devices with their start and end apart: 14, of which 12 were waited for; matrix products, arithmetic and copies ran while one was open for 18% of the time, Pallas kernels for 0%

commit v1 on v0

--- a/solution.py
+++ b/solution.py
@@ -78,7 +78,9 @@
 def fetch_mlp(w_in, w_mlp_out, gain_mlp):
     return (
         lax.all_gather(w_in, "dp", axis=0, tiled=True),
-        lax.all_gather(w_mlp_out, "dp", axis=1, tiled=True),
+        jnp.concatenate(
+            lax.all_to_all(jnp.stack([w_mlp_out] * lax.axis_size("dp")), "dp", 0, 0), axis=1
+        ),
         lax.all_gather(gain_mlp, "dp", axis=0, tiled=True),
     )
 

time: 888 us -> 894 us (level)
  waiting for transfers between devices: 458 us -> 433 us
  blocking collectives: 182 us -> 194 us
    all_gather x1, waiting for transfers between devices: 20.7 us -> 5.8 us  [fetch_mlp(): lax.all_gather(w_in, 'dp', axis=0, tiled=True)]
    all_gather x1, blocking collectives: 51 us -> 63.1 us  [fetch_mlp_again(): lax.all_gather(w_mlp_out, 'dp', axis=1, tiled=True)]
  transfers between devices with their start and end apart: 14 -> 15, of which waited for: 12 -> 12; matrix products, arithmetic and copies ran while one was open for 18% -> 20% of each run, Pallas kernels for 0% -> 0%
where the time goes in v1:
time: 894 us; the launch traced here: 881 us
  waiting for transfers between devices  433 us (48%)
  blocking collectives  194 us (22%)
  matrix products  115 us (13%)
  local copies, waits for them, and re-layouts  58.4 us (7%)
  other arithmetic  55 us (6%)
  between operations  16.4 us (2%)
    reduce_scatter x1, waiting for transfers between devices, shards(): lax.psum_scatter(grad_qkv, 'dp', scatter_dimension=0, tiled=True)  139 us
    reduce_scatter x1, waiting for transfers between devices, shards(): lax.psum_scatter(grad_attn_out, 'dp', scatter_dimension=1, tiled=True)  129 us
    unnamed x2, blocking collectives  86.3 us
    reduce_scatter x1, waiting for transfers between devices, shards(): lax.psum_scatter(grad_mlp_out, 'dp', scatter_dimension=1, tiled=True)  80.4 us
    all_gather x1, blocking collectives, fetch_mlp_again(): lax.all_gather(w_mlp_out, 'dp', axis=1, tiled=True)  63.1 us
    all_gather x1, blocking collectives, fetch_attention(): lax.all_gather(w_attn_out, 'dp', axis=1, tiled=True)  41.6 us
    dynamic_update_slice x4, local copies, waits for them, and re-layouts, attention_forward(): lax.map(one_block, (queries.reshape(block_count, block_rows, heads_here,...  31.5 us
    all_gather x1, waiting for transfers between devices, fetch_attention(): lax.all_gather(w_qkv, 'dp', axis=0, tiled=True)  25.5 us
  transfers between devices with their start and end apart: 15, of which 12 were waited for; matrix products, arithmetic and copies ran while one was open for 20% of the time, Pallas kernels for 0%

profile of v1, /device:TPU:0, one launch (start us, length us, event | category | flops | bytes accessed | tf_op | source)
XLA Modules:
  0.0 880.7 jit_solution(18129527226678899810)
XLA Ops:
  11.2 43.5 %all-reduce.6 = (bf16[768]{0:T(1024)(128)(2,1)S(1)}, bf16[768]{0:T(1024)(128)(2,1)S(1)}) all-reduce(bf16[768]{0:T(1024)(128)(2,1)S(1)} %dynamic-update-slice, bf16[768]{0:T(1024)(128)(2,1)S(1)} %dynamic-update-slice.1), channel_id=1, replica_groups=mesh['dp'=16,'tensor'=2] {'dp'}, use_global_device_ids=true, to_apply=%add | all-reduce | flops 1536 | bytes 6144
  57.4 41.6 %all_gather.38 = bf16[384,768]{0,1:T(8,128)(2,1)} all-gather(bf16[384,48]{0,1:T(8,128)(2,1)S(1)} %copy-done.33), channel_id=1, replica_groups=mesh['dp'=16,'tensor'=2] {'dp'}, dimensions={1}, use_global_device_ids=true | all-gather | bytes 626688 | tf_op jit(solution)/shard_map/all_gather | solution.py:65
  99.1 25.5 %all-gather.9.cloned.1.call-done = bf16[768,3,384]{2,0,1:T(8,128)(2,1)} async-done(((bf16[48,3,384]{2,0,1:T(8,128)(2,1)}), bf16[768,3,384]{2,0,1:T(8,128)(2,1)}) %all-gather.9.cloned.1.call-update) | async-done | bytes 1769488 | tf_op jit(solution)/shard_map/all_gather | solution.py:64
  132.2 25.0 %while.27 = (s32[]{:T(128)}, bf16[2,512,6,64]{1,3,2,0:T(8,128)(2,1)S(1)}, f32[2,6,512]{2,1,0:T(8,128)S(1)}, s32[2,512]{1,0:T(2,128)S(1)}, s32[1024]{0:T(1024)S(1...) while((s32[]{:T(128)}, ...), condition=%wide.region_6.7_spmd, body=%wide.region_3.6_spmd.sunk | while | flops 843576320 | bytes 42727540 | solution.py:159
  139.6 5.1 fusion.174
  152.1 5.1 fusion.174
  173.9 7.2 all-to-all-start
  181.2 63.1 %all_gather.43 = bf16[576,768]{0,1:T(8,128)(2,1)} all-gather(bf16[576,48]{0,1:T(8,128)(2,1)S(1)} %copy-done.25), channel_id=1, replica_groups=mesh['dp'=16,'tensor'=2] {'dp'}, dimensions={1}, use_global_device_ids=true | all-gather | bytes 940032 | tf_op jit(solution)/shard_map/all_gather | solution.py:91
  247.2 5.8 all-gather.13.cloned.1.call-done
  252.9 11.3 %all-gather.11.cloned.1.call-done = bf16[1024,768]{1,0:T(8,128)(2,1)} async-done(((bf16[512,768]{1,0:T(8,128)(2,1)}), bf16[1024,768]{1,0:T(8,128)(2,1)}) %all-gather.11.cloned.1.call-update) | async-done | bytes 1572880 | tf_op jit(solution)/shard_map/all_gather | solution.py:97
  268.3 5.6 fusion.86
  280.5 9.4 %convolution_convert_fusion = bf16[1024,768]{1,0:T(8,128)(2,1)} fusion(bf16[576,768]{0,1:T(8,128)(2,1)} %bitcast.15, f32[1024,2,576]{0,2,1:T(8,128)} %copy-done.6), kind=kOutput, calls=%fused_computation.111 | convolution fusion | flops 945684480 | bytes 7176192 | tf_op jit(solution)/shard_map/dot_general | solution.py:107
  294.0 9.4 %reduce-scatter.11.cloned.1.call-done = bf16[512,768]{1,0:T(8,128)(2,1)} async-done(((bf16[1024,768]{1,0:T(8,128)(2,1)}), bf16[512,768]{1,0:T(8,128)(2,1)}) %reduce-scatter.11.cloned.1.call-update) | async-done | bytes 786448 | tf_op jit(solution)/shard_map/reduce_scatter | solution.py:109
  309.3 5.9 fusion.73
  328.3 89.5 %while.28 = (s32[]{:T(128)}, f32[1024,6,64]{0,2,1:T(8,128)S(1)}, f32[1024,6,64]{0,2,1:T(8,128)}, f32[2,512,6,64]{1,0,3,2:T(2,128)}, bf16[2,512,6,64]{1,3,2,0:T(8...) while((s32[]{:T(128)}, f32[1024,6,64]{0,2,1:T(8,128)S(1)}, ...), condition=%wide.region_16.17_spmd.clone, body=%wide.region_14.16_spmd.clone.sunk | while | flops 2063135744 | bytes 110721200 | solution.py:210
  331.7 5.5 bitcast_add_fusion.5
  337.2 8.5 multiply_reduce_fusion.4
  345.6 7.0 multiply_convert_fusion.5
  357.8 14.9 %dynamic_update_slice.19 = f32[2,512,6,64]{1,0,3,2:T(2,128)} dynamic-update-slice(f32[2,512,6,64]{1,0,3,2:T(2,128)} %get-tuple-element.473, f32[1,512,6,64]{1,0,3,2:T(1,128)S(1)} %copy.89, s32[]{:T(128)S(6)} %copy.109, s32[]{:T(128)} %constant.64.clone.1..sunk, s32[]{:T(128)} %constant.64.clone.1..sunk, s32[]{:T(128)} %constant.64.clone.1..sunk) | dynamic-update-slice | bytes 1572868 | tf_op jit(solution)/shard_map/while/body/jit(dynamic_update_index_in_dim)/dynamic_update_slice | solution.py:159
  376.0 6.1 bitcast_add_fusion.5
  382.0 8.5 multiply_reduce_fusion.4
  390.5 6.9 multiply_convert_fusion.5
  402.7 14.9 %dynamic_update_slice.19 = f32[2,512,6,64]{1,0,3,2:T(2,128)} dynamic-update-slice(f32[2,512,6,64]{1,0,3,2:T(2,128)} %get-tuple-element.473, f32[1,512,6,64]{1,0,3,2:T(1,128)S(1)} %copy.89, s32[]{:T(128)S(6)} %copy.109, s32[]{:T(128)} %constant.64.clone.1..sunk, s32[]{:T(128)} %constant.64.clone.1..sunk, s32[]{:T(128)} %constant.64.clone.1..sunk) | dynamic-update-slice | bytes 1572868 | tf_op jit(solution)/shard_map/while/body/jit(dynamic_update_index_in_dim)/dynamic_update_slice | solution.py:159
  428.4 5.7 bitcast_convert_fusion
  434.2 5.7 fusion.82
  443.8 5.4 fusion.77
  450.0 12.5 %reduce-scatter.21.cloned.1.call-done = f32[48,2,576]{2,0,1:T(8,128)} async-done(((f32[768,2,576]{2,0,1:T(8,128)}), f32[48,2,576]{2,0,1:T(8,128)}) %reduce-scatter.21.cloned.1.call-update) | async-done | bytes 221200 | tf_op jit(solution)/shard_map/reduce_scatter | solution.py:269
  464.2 9.5 %reduce-scatter.15.cloned.1.call-done = bf16[512,768]{1,0:T(8,128)(2,1)} async-done(((bf16[1024,768]{1,0:T(8,128)(2,1)}), bf16[512,768]{1,0:T(8,128)(2,1)}) %reduce-scatter.15.cloned.1.call-update) | async-done | bytes 786448 | tf_op jit(solution)/shard_map/reduce_scatter | solution.py:122
  476.3 42.8 %all-reduce.4 = (f32[768]{0:T(1024)S(1)}, f32[768]{0:T(1024)S(1)}) all-reduce(f32[768]{0:T(1024)S(1)} %get-tuple-element.227, f32[768]{0:T(1024)S(1)} %copy-done.40), channel_id=10, replica_groups=mesh['dp'=16,'tensor'=2] {'dp'}, use_global_device_ids=true, to_apply=%region_25.26.clone | all-reduce | flops 1536 | bytes 12288
  525.8 80.4 %reduce-scatter.23.cloned.1.call-done = f32[576,48]{0,1:T(8,128)} async-done(((f32[576,768]{0,1:T(8,128)}), f32[576,48]{0,1:T(8,128)}) %reduce-scatter.23.cloned.1.call-update) | async-done | bytes 110608 | tf_op jit(solution)/shard_map/reduce_scatter | solution.py:270
  606.3 128.6 %reduce-scatter.19.cloned.1.call-done = f32[384,48]{0,1:T(8,128)} async-done(((f32[384,768]{0,1:T(8,128)}), f32[384,48]{0,1:T(8,128)}) %reduce-scatter.19.cloned.1.call-update) | async-done | bytes 73744 | tf_op jit(solution)/shard_map/reduce_scatter | solution.py:309
  734.9 138.9 %reduce-scatter.17.cloned.1.call-done = f32[48,3,384]{2,0,1:T(8,128)} async-done(((f32[768,3,384]{2,0,1:T(8,128)}), f32[48,3,384]{2,0,1:T(8,128)}) %reduce-scatter.17.cloned.1.call-update) | async-done | bytes 221200 | tf_op jit(solution)/shard_map/reduce_scatter | solution.py:308
  (220 shorter events, 123.5 us)
Async XLA Ops:
  7.2 91.8 %all-gather.7.cloned.1.call-start = ((), (), s32[]{:S(2)}) async-start(), calls=%async_computation.9 | async-start | bytes 2359296 | tf_op jit(solution)/shard_map/all_gather | solution.py:97
  9.1 46.8 %copy-start.31 = (f32[512]{0:T(512)}, f32[512]{0:T(512)S(1)}, u32[]{:S(2)}) copy-start(f32[512]{0:T(512)S(1)} %broadcast_multiply_fusion.1) | copy-start | bytes 6148
  9.1 47.6 %copy-start.42 = (s32[1,16]{1,0:T(1,128)S(1)}, s32[1,16]{1,0:T(1,128)}, u32[]{:S(2)}) copy-start(s32[1,16]{1,0:T(1,128)} %param.14) | copy-start | bytes 196
  9.1 48.3 %copy-start.33 = (bf16[384,48]{0,1:T(8,128)(2,1)S(1)}, bf16[384,48]{0,1:T(8,128)(2,1)}, u32[]{:S(2)}) copy-start(bf16[384,48]{0,1:T(8,128)(2,1)} %param.16) | copy-start | bytes 110596
  9.4 45.3 %copy-start.38 = (f32[512]{0:T(512)}, f32[512]{0:T(512)S(1)}, u32[]{:S(2)}) copy-start(f32[512]{0:T(512)S(1)} %multiply_reduce_fusion.2) | copy-start | bytes 6148
  9.4 47.4 %copy-start.34 = (f32[512]{0:T(512)}, f32[512]{0:T(512)S(1)}, u32[]{:S(2)}) copy-start(f32[512]{0:T(512)S(1)} %fusion.89) | copy-start | bytes 6148
  55.9 68.7 %all-gather.9.cloned.1.call-start = ((), (), s32[]{:S(2)}) async-start(), calls=%async_computation.10 | async-start | bytes 1880064 | tf_op jit(solution)/shard_map/all_gather | solution.py:64
  56.6 112.6 %reduce-scatter.9.cloned.1.call-start = ((), (), s32[]{:S(2)}) async-start(), calls=%async_computation.11 | async-start | bytes 2359296 | tf_op jit(solution)/shard_map/reduce_scatter | solution.py:109
  57.4 72.6 %copy-start.11 = (f32[1024,32]{0,1:T(8,128)}, f32[1024,32]{0,1:T(8,128)S(1)}, u32[]{:S(2)}) copy-start(f32[1024,32]{0,1:T(8,128)S(1)} %get-tuple-element.300) | copy-start | bytes 393220
  57.4 72.6 %copy-start.13 = (f32[1024,32]{0,1:T(8,128)}, f32[1024,32]{0,1:T(8,128)S(1)}, u32[]{:S(2)}) copy-start(f32[1024,32]{0,1:T(8,128)S(1)} %get-tuple-element.301) | copy-start | bytes 393220
  161.2 83.1 %all-gather.15.cloned.1.call-start = ((), (), s32[]{:S(2)}) async-start(), calls=%async_computation.15 | async-start | bytes 2359296 | tf_op jit(solution)/shard_map/all_gather | solution.py:101
  163.7 89.3 %all-gather.13.cloned.1.call-start = ((), (), s32[]{:S(2)}) async-start(), calls=%async_computation.13 | async-start | bytes 2088960 | tf_op jit(solution)/shard_map/all_gather | solution.py:80
  164.4 99.8 %all-gather.11.cloned.1.call-start = ((), (), s32[]{:S(2)}) async-start(), calls=%async_computation.12 | async-start | bytes 2359296 | tf_op jit(solution)/shard_map/all_gather | solution.py:97
  173.9 106.6 %all-to-all-start = ((bf16[16,576,48]{1,2,0:T(8,128)(2,1)}), bf16[16,576,48]{1,2,0:T(8,128)(2,1)}, u32[]{:S(2)}, u32[]{:S(2)}) async-start(bf16[16,576,48]{1,2,0:T(8,128)(2,1)} %stack.19), calls=%async_computation.1 | async-start | bytes 1966080 | tf_op jit(solution)/shard_map/all_to_all | solution.py:82
  181.1 109.7 %reduce-scatter.13.cloned.1.call-start = ((), (), s32[]{:S(2)}) async-start(), calls=%async_computation.16 | async-start | bytes 2359296 | tf_op jit(solution)/shard_map/reduce_scatter | solution.py:122
  280.5 22.9 %reduce-scatter.11.cloned.1.call-start = ((), (), s32[]{:S(2)}) async-start(), calls=%async_computation.14 | async-start | bytes 2359296 | tf_op jit(solution)/shard_map/reduce_scatter | solution.py:109
  290.0 30.0 %all-gather.17.cloned.1.call-start = ((), (), s32[]{:S(2)}) async-start(), calls=%async_computation.17 | async-start | bytes 2359296 | tf_op jit(solution)/shard_map/all_gather | solution.py:101
  291.4 12.0 %copy-start.10 = (bf16[512,768]{1,0:T(8,128)(2,1)S(1)}, bf16[512,768]{1,0:T(8,128)(2,1)}, u32[]{:S(2)}) copy-start(bf16[512,768]{1,0:T(8,128)(2,1)} %reduce-scatter.13.cloned.1.call-done) | copy-start | bytes 2359300
  308.8 153.7 %reduce-scatter.21.cloned.1.call-start = ((), (), s32[]{:S(2)}) async-start(), calls=%async_computation.21 | async-start | bytes 4177920 | tf_op jit(solution)/shard_map/reduce_scatter | solution.py:269
  315.2 158.6 %reduce-scatter.15.cloned.1.call-start = ((), (), s32[]{:S(2)}) async-start(), calls=%async_computation.18 | async-start | bytes 2359296 | tf_op jit(solution)/shard_map/reduce_scatter | solution.py:122
  428.4 5.8 copy-start.5
  434.2 5.9 copy-start.19
  434.2 172.1 %reduce-scatter.23.cloned.1.call-start = ((), (), s32[]{:S(2)}) async-start(), calls=%async_computation.22 | async-start | bytes 2088960 | tf_op jit(solution)/shard_map/reduce_scatter | solution.py:270
  440.0 294.9 %reduce-scatter.19.cloned.1.call-start = ((), (), s32[]{:S(2)}) async-start(), calls=%async_computation.20 | async-start | bytes 1253376 | tf_op jit(solution)/shard_map/reduce_scatter | solution.py:309
  443.7 430.1 %reduce-scatter.17.cloned.1.call-start = ((), (), s32[]{:S(2)}) async-start(), calls=%async_computation.19 | async-start | bytes 3760128 | tf_op jit(solution)/shard_map/reduce_scatter | solution.py:308
  449.2 24.5 %copy-start.1 = (f32[512,768]{1,0:T(8,128)S(1)}, f32[512,768]{1,0:T(8,128)}, u32[]{:S(2)}) copy-start(f32[512,768]{1,0:T(8,128)} %param.13) | copy-start | bytes 4718596
  449.2 24.5 %copy-start.30 = (f32[768]{0:T(1024)S(1)}, f32[768]{0:T(1024)}, u32[]{:S(2)}) copy-start(f32[768]{0:T(1024)} %copy-done.29) | copy-start | bytes 9220
  449.2 24.5 %copy-start.32 = (f32[512]{0:T(512)S(1)}, f32[512]{0:T(512)}, u32[]{:S(2)}) copy-start(f32[512]{0:T(512)} %copy-done.31) | copy-start | bytes 6148
  449.2 26.1 %copy-start.39 = (f32[512]{0:T(512)S(1)}, f32[512]{0:T(512)}, u32[]{:S(2)}) copy-start(f32[512]{0:T(512)} %copy-done.38) | copy-start | bytes 6148
  449.2 26.1 %copy-start.35 = (f32[512]{0:T(512)S(1)}, f32[512]{0:T(512)}, u32[]{:S(2)}) copy-start(f32[512]{0:T(512)} %copy-done.34) | copy-start | bytes 6148
  464.2 12.0 %copy-start.40 = (f32[768]{0:T(1024)S(1)}, f32[768]{0:T(1024)}, u32[]{:S(2)}) copy-start(f32[768]{0:T(1024)} %get-tuple-element.229) | copy-start | bytes 9220
  464.2 57.9 %copy-start.37 = (f32[512]{0:T(512)S(1)}, f32[512]{0:T(512)}, u32[]{:S(2)}) copy-start(f32[512]{0:T(512)} %copy-done.36) | copy-start | bytes 6148
  (29 other events, 79.1 us)
Sparse Core Ops, SparseCore 0:
  56.0 5.6 all-gather.6
  64.4 60.1 all-gather.8
  161.3 7.8 reduce-scatter.8
  170.7 10.9 all-gather.14
  185.2 67.7 all-gather.12
  255.0 9.1 all-gather.10
  280.6 10.2 reduce-scatter.12
  293.1 10.2 reduce-scatter.10
  308.9 10.9 all-gather.16
  325.7 136.7 reduce-scatter.20
  465.4 8.2 reduce-scatter.14
  479.0 127.2 reduce-scatter.22
  612.3 122.5 reduce-scatter.18
  741.3 132.5 reduce-scatter.16
